TPU v7x, 32 devices: a whole 2x2x4 slice. The times are simulated.
32 devices in a mesh: groups: 2 (over x), srv: 16 (over z, y, core).
Axes of the slice: x: 2, y: 2, z: 4, core: 2. Of those that a mesh axis runs over, the one named last changes fastest.
Arguments:
- fields: bfloat16 [384, 336, 128], P(('groups', 'srv')), parts along dimension 0, may hold values from -6 to 6
- tile_count: int32 [192], P('srv'), may hold values from 32 to 128
- route: int32 [16, 16, 2], P('srv'), may hold values from 0 to 11, as said below
- weights: bfloat16 [9216, 128, 128], P('srv'), may hold values from -0.1875 to 0.1875
- block_src: int32 [9216], P('srv'), may hold values from 0 to 31, as said below
- destination_block: int32 [9216], P('srv'), may hold values from 0 to 255, as said below
- block_live: int32 [9216], P('srv'), may hold values from 0 to 1, as said below
Outputs:
- remapped: bfloat16 [512, 336, 128], P(('groups', 'srv')), parts along dimension 0
There are 2 independent parts, one for each index of `groups`. A program takes and returns all parts, laid end to end along the dimension named above; an argument that names none is the same for every part. Nothing has to cross between parts.
Inputs may be any that keep to these rules, and one draw needn't show every extreme that they name: route[s, d] lists 2 different blocks of compute rank d, as indices among its 12 blocks; every server needs exactly 2 blocks of every rank. block_src[k] = d * 2 + j names entry j of route[s, d] for the slot's server s = k // 576. `destination_block`: a slot of server s adds to one of the destination blocks (s * 16 + i) % 256 with 0 <= i <= 16: its own band or the first block of the next server's band. `block_live`: the live slots of each server come first among its 576 slots; some server has all of them live.
All inputs are finite; a program needn't handle non-finite values.
Results may differ from a plain program's by a relative error of at most 0.001.
Values may be sent and summed in bfloat16 or wider, within the bound.
A program may use at most 128 MiB of HBM per device.

v0:
```python
import functools

import jax
import jax.numpy as jnp
from jax import lax
from jax.experimental import pallas as pl
from jax.experimental.pallas import tpu as pltpu
from jax.sharding import PartitionSpec as P

DB_DEV = 16
UNIT = 8
RING = 12
LIMIT = 54 << 20


def plan(bucket, valid, n_buckets, source, steps_max):
    slots = bucket.shape[0]
    zero_source = -1
    ids = jnp.arange(n_buckets, dtype=jnp.int32)
    member = (bucket[None, :] == ids[:, None]) & valid[None, :]
    steps = (jnp.sum(member.astype(jnp.int32), axis=1) + UNIT - 1) // UNIT
    edges = jnp.arange(n_buckets + 1, dtype=jnp.int32)
    starts = jnp.sum(jnp.where(ids[None, :] < edges[:, None], steps[None, :], 0), axis=1)
    index = jnp.arange(slots, dtype=jnp.int32)
    before = jnp.sum(
        ((bucket[None, :] == bucket[:, None]) & valid[None, :] & (index[None, :] < index[:, None])).astype(jnp.int32),
        axis=1,
    )
    own = jnp.sum(jnp.where(ids[None, :] < bucket[:, None], steps[None, :], 0), axis=1)
    place = jnp.where(valid, own * UNIT + before, -1)
    places = jnp.arange(steps_max * UNIT, dtype=jnp.int32)
    hit = places[:, None] == place[None, :]
    slot = jnp.sum(jnp.where(hit, (index + jnp.where(before == 0, slots, 0))[None, :], 0), axis=1)
    src = jnp.sum(jnp.where(hit, source[None, :] - zero_source, 0), axis=1) + zero_source
    return starts, slot, src


def contract(blocks, factors):
    return lax.dot_general(
        jnp.concatenate(blocks, axis=1),
        jnp.concatenate(factors, axis=1),
        (((1,), (1,)), ((), ())),
        preferred_element_type=jnp.float32,
    )


def exchange_kernel(
    n, steps, tile_count, starts, slot, src,
    wanted, fields, w_hbm,
    near, far, totals, shared,
    asked, asked_now, outgoing, held, prefix,
    ask_send, ask_recv, send_sem, recv_sem, own_sem, w_sem,
):
    me = lax.axis_index("srv")
    half = n // 2
    rows, width = fields.shape[1:]
    capacity = outgoing.shape[1]
    blocks = half * capacity
    load = pltpu.make_async_copy(w_hbm, held, w_sem)
    load.start()

    def partner(i):
        return lax.rem(me + half + ((i + 1) // 2) * (2 * ((i + 1) % 2) - 1), n)

    barrier = pltpu.get_barrier_semaphore()

    def greet(i, carry):
        pl.semaphore_signal(barrier, inc=1, device_id={"srv": partner(i)}, device_id_type=pl.DeviceIdType.MESH)
        return carry

    lax.fori_loop(0, n - 1, greet, 0)
    pl.semaphore_wait(barrier, n - 1)

    def ask(i, carry):
        pltpu.make_async_remote_copy(
            src_ref=wanted.at[partner(i)], dst_ref=asked.at[me], send_sem=ask_send.at[i], recv_sem=ask_recv.at[me],
            device_id={"srv": partner(i)}, device_id_type=pl.DeviceIdType.MESH,
        ).start()
        return carry

    lax.fori_loop(0, n - 1, ask, 0)
    own = pltpu.make_async_copy(wanted.at[me], asked.at[me], own_sem)
    own.start()
    own.wait()
    near[blocks] = jnp.zeros((rows, width), near.dtype)
    far[blocks] = jnp.zeros((rows, width), far.dtype)

    def heard(i, carry):
        peer = partner(i)
        pltpu.make_async_copy(asked.at[peer], asked.at[peer], ask_recv.at[peer]).wait()
        pltpu.make_async_copy(wanted.at[peer], wanted.at[peer], ask_send.at[i]).wait()
        return carry

    lax.fori_loop(0, n - 1, heard, 0)
    local = pltpu.make_async_copy(asked, asked_now, own_sem)
    local.start()
    local.wait()
    cells = lax.broadcasted_iota(jnp.int32, (rows, width), 1)

    def chosen(peer, j):
        block = asked_now[peer, 0, j]
        return jnp.where(cells < tile_count[block], fields[block].astype(jnp.float32), 0.0).astype(fields.dtype)

    def send(i, carry):
        peer = partner(i)
        for j in range(capacity):
            outgoing[i, j] = chosen(peer, j)

        def start(target):
            pltpu.make_async_remote_copy(
                src_ref=outgoing.at[i], dst_ref=target.at[pl.ds(lax.rem(me, half) * capacity, capacity)],
                send_sem=send_sem.at[i], recv_sem=recv_sem.at[me],
                device_id={"srv": peer}, device_id_type=pl.DeviceIdType.MESH,
            ).start()

        @pl.when(peer // half == me // half)
        def _():
            start(near)

        @pl.when(peer // half != me // half)
        def _():
            start(far)

        return carry

    lax.fori_loop(0, n - 1, send, 0)
    for j in range(capacity):
        near[lax.rem(me, half) * capacity + j] = chosen(me, j)

    def arrive(target, i, first):
        piece = target.at[pl.ds(i * capacity, capacity)]
        pltpu.make_async_copy(piece, piece, recv_sem.at[first + i]).wait()

    def arrive_near(i, carry):
        @pl.when(i != lax.rem(me, half))
        def _():
            arrive(near, i, (me // half) * half)

        return carry

    lax.fori_loop(0, half, arrive_near, 0)
    load.wait()
    prefix[0] = jnp.zeros((rows, width), jnp.float32)
    slots, n_rows, last_step = w_hbm.shape[0], totals.shape[0] + 1, slot.shape[0] // UNIT - 1

    def run(x, phase):
        base, end = starts[phase * n_rows], starts[(phase + 1) * n_rows]

        def step(q, carry):
            real = base + q < end
            p = jnp.minimum(base + q, last_step) * UNIT
            places = [src[p + u] for u in range(UNIT)]
            places = [jnp.where(real & (s >= 0), s - phase * blocks, blocks) for s in places]
            part = contract([x[s] for s in places], [held[lax.rem(slot[p + u], slots)] for u in range(UNIT)])
            prefix[q + 1] = jnp.where(slot[p] < slots, prefix[q], 0.0) + part
            return carry

        lax.fori_loop(0, steps, step, 0)

    def sums(g, phase):
        base = starts[phase * n_rows]
        low = jnp.minimum(starts[phase * n_rows + g] - base, steps)
        high = jnp.minimum(starts[phase * n_rows + g + 1] - base, steps)
        return jnp.where(high > low, prefix[high], 0.0)

    run(near, 0)

    def pick(g, carry):
        totals[g] = sums(g, 0)
        return carry

    lax.fori_loop(0, n_rows - 1, pick, 0)
    shared[...] = sums(n_rows - 1, 0)

    def finish(i, carry):
        pltpu.make_async_copy(outgoing.at[i], outgoing.at[i], send_sem.at[i]).wait()
        return carry

    def arrive_far(i, carry):
        arrive(far, i, (1 - me // half) * half)
        return carry

    lax.fori_loop(0, half, arrive_far, 0)
    lax.fori_loop(0, n - 1, finish, 0)


def exchange(n, n_rows, steps, tile_count, starts, slot, src, route, fields, weights):
    rows, width = fields.shape[1:]
    capacity = route.shape[1]
    blocks = n // 2 * capacity
    smem = pl.BlockSpec(memory_space=pltpu.SMEM)
    vmem = pl.BlockSpec(memory_space=pltpu.VMEM)
    hbm = pl.BlockSpec(memory_space=pl.ANY)
    wanted = jnp.broadcast_to(jnp.pad(route, ((0, 0), (0, 128 - capacity)))[:, None, :], (n, 8, 128))
    dma = pltpu.SemaphoreType.DMA
    return pl.pallas_call(
        functools.partial(exchange_kernel, n, steps),
        out_shape=[
            jax.ShapeDtypeStruct((blocks + 1, rows, width), fields.dtype),
            jax.ShapeDtypeStruct((blocks + 1, rows, width), fields.dtype),
            jax.ShapeDtypeStruct((n_rows - 1, rows, width), jnp.float32),
            jax.ShapeDtypeStruct((rows, width), jnp.float32),
        ],
        in_specs=[smem] * 4 + [vmem] * 2 + [hbm],
        out_specs=[vmem] * 4,
        scratch_shapes=[
            pltpu.VMEM((n, 8, 128), jnp.int32),
            pltpu.SMEM((n, 8, 128), jnp.int32),
            pltpu.VMEM((n - 1, capacity, rows, width), fields.dtype),
            pltpu.VMEM(weights.shape, weights.dtype),
            pltpu.VMEM((steps + 1, rows, width), jnp.float32),
            dma((n - 1,)),
            dma((n,)),
            dma((n - 1,)),
            dma((n,)),
            dma,
            dma,
        ],
        compiler_params=pltpu.CompilerParams(
            vmem_limit_bytes=LIMIT, collective_id=0, has_side_effects=True
        ),
    )(tile_count, starts, slot, src, wanted, fields, weights)


def product_kernel(first, last, n_rows, done, finish, starts, slot, src, near, far, w_hbm, prev, *refs):
    *outs, ring, acc, w_sem = refs
    zero = far.shape[0] - 1
    begin, end = starts[n_rows + first], starts[n_rows + last]

    def fetch(p, at):
        for u in range(UNIT):
            pltpu.make_async_copy(w_hbm.at[lax.rem(slot[p * UNIT + u], w_hbm.shape[0])], ring.at[at, u], w_sem.at[at]).start()

    def step(x, p, at):
        pltpu.make_async_copy(ring.at[at], ring.at[at], w_sem.at[at]).wait()
        places = [src[p * UNIT + u] for u in range(UNIT)]
        acc[...] += contract([x[jnp.where(s < 0, zero, lax.rem(s, zero))] for s in places], [ring[at, u] for u in range(UNIT)])

    def left_over(p, carry):
        fetch(p, RING)
        step(near, p, RING)
        return carry

    def prime(p, carry):
        fetch(p, lax.rem(p, RING))
        return carry

    def far_step(p, carry):
        step(far, p, lax.rem(p, RING))

        @pl.when(p + RING < end)
        def _():
            fetch(p + RING, lax.rem(p, RING))

        return carry

    lax.fori_loop(begin, jnp.minimum(end, begin + RING), prime, 0)

    def bucket(g, carry):
        acc[...] = prev[g - first]
        lax.fori_loop(jnp.maximum(starts[g], done), starts[g + 1], left_over, 0)
        lax.fori_loop(starts[n_rows + g], starts[n_rows + g + 1], far_step, 0)
        finish(g - first, acc, outs)
        return carry

    lax.fori_loop(first, last, bucket, 0)


def products(starts, slot, src, near, far, w, prev, first, last, n_rows, done, finish, out_shape):
    rows, width = near.shape[1:]
    smem = pl.BlockSpec(memory_space=pltpu.SMEM)
    hbm = pl.BlockSpec(memory_space=pl.ANY)
    vmem = pl.BlockSpec(memory_space=pltpu.VMEM)
    n_slots = w.shape[0] * (last - first) // (2 * n_rows)
    return pl.pallas_call(
        functools.partial(product_kernel, first, last, n_rows, done, finish),
        out_shape=out_shape,
        in_specs=[smem] * 3 + [vmem] * 2 + [hbm, vmem],
        out_specs=jax.tree.map(lambda _: vmem, out_shape),
        scratch_shapes=[
            pltpu.VMEM((RING + 1, UNIT, width, width), w.dtype),
            pltpu.VMEM((rows, width), jnp.float32),
            pltpu.SemaphoreType.DMA((RING + 1,)),
        ],
        compiler_params=pltpu.CompilerParams(vmem_limit_bytes=LIMIT),
        cost_estimate=pl.CostEstimate(
            flops=4 * n_slots * rows * width * width, bytes_accessed=4 * n_slots * width * width, transcendentals=0
        ),
    )(starts, slot, src, near, far, w, prev)


def finish_rows(i, total, outs):
    out, head = outs

    @pl.when(i == 0)
    def _():
        head[...] = total[...]

    out[i] = total[...].astype(out.dtype)


def finish_excess(i, total, outs):
    outs[0][...] = total[...]


def shards(fields, tile_count, route, weights, block_src, destination_block, block_live):
    servers = lax.axis_size("srv")
    server = lax.axis_index("srv")
    held, rows, width = fields.shape
    slots = weights.shape[0]
    capacity = route.shape[2]
    band = DB_DEV
    n_rows = band + 1
    half = servers // 2
    blocks = half * capacity
    local = jnp.mod(destination_block - server * band, band * servers)
    entry, rank = block_src % capacity, block_src // capacity
    phase = (rank // half != server // half).astype(jnp.int32)
    source = phase * blocks + (rank % half) * capacity + entry
    steps_max = -(-slots // UNIT) + 2 * n_rows
    starts, slot, src = plan(phase * n_rows + local, block_live == 1, 2 * n_rows, source, steps_max)
    done = slots // UNIT // 2 + n_rows
    near, far, totals, shared = exchange(
        servers, n_rows, done, tile_count, starts, slot, src, route[0], fields, weights
    )
    operands = (starts, slot, src, near, far, weights)
    piece = jax.ShapeDtypeStruct((rows, width), jnp.float32)
    common = (n_rows, done)
    (excess,) = products(*operands, shared[None], band, n_rows, *common, finish_excess, (piece,))
    arrived = lax.ppermute(excess, "srv", [(i, (i + 1) % servers) for i in range(servers)])
    body = jax.ShapeDtypeStruct((band, rows, width), jnp.bfloat16)
    out, head = products(*operands, totals, 0, band, *common, finish_rows, (body, piece))
    return out.at[0].set((head + arrived).astype(jnp.bfloat16))


def solution(mesh):
    in_specs = (
        P(("groups", "srv"), None, None),
        P("srv"),
        P("srv", None, None),
        P("srv", None, None),
        P("srv"),
        P("srv"),
        P("srv"),
    )
    out_specs = P(("groups", "srv"), None, None)
    return jax.shard_map(shards, mesh=mesh, in_specs=in_specs, out_specs=out_specs, check_vma=False)
```

profile of v0, /device:TPU:7, one launch (start us, length us, event | category | flops | bytes accessed | tf_op | source)
XLA Modules:
  0.0 114.5 jit_solution(14723807855707717438)
XLA Ops:
  0.0 0.7 broadcast_compare_fusion
  0.7 0.7 fusion.10
  1.4 0.7 fusion.6
  2.1 0.1 convert_reduce_fusion.1
  2.2 0.3 convert_reduce_fusion
  2.6 0.6 select_reduce_fusion.3.starts
  3.2 0.1 select_reduce_fusion.2
  3.3 0.7 select_add_fusion
  4.0 1.1 select_reduce_fusion
  5.1 0.6 broadcast_add_fusion.src
  5.7 0.8 copy.10
  6.4 0.6 broadcast_in_dim.85.wanted
  7.1 62.8 %shard_map.73 = (bf16[17,336,128]{2,1,0:T(8,128)(2,1)}, bf16[17,336,128]{2,1,0:T(8,128)(2,1)}, f32[16,336,128]{2,1,0:T(8,128)}, f32[336,128]{1,0:T(8,128)}) custom-call(s32[12]{0:T(128)} %tile_count.1, s32[35]{0:T(128)} %select_reduce_fusion.3.starts, s32[848]{0:T(1024)} %get-tuple-element.30.slot, s32[848]{0:T(1024)} %broadcast_add_fusion.src, ...), custom_call_target="tpu_custom_call" | custom-call | tf_op jit(solution)/shard_map/pallas_call | solution.py:196
  69.9 4.2 %shard_map.75 = f32[336,128]{1,0:T(8,128)} custom-call(s32[35]{0:T(128)} %select_reduce_fusion.3.starts, s32[848]{0:T(1024)} %get-tuple-element.30.slot, s32[848]{0:T(1024)} %broadcast_add_fusion.src, bf16[17,336,128]{2,1,0:T(8,128)(2,1)} %get-tuple-element.23.near, bf16[17,336,128]{2,1,0:T(8,128)(2,1)} %get-tuple-element.24.far, ...), custom_call_target="tpu_custom_call" | custom-call | flops 352321536 | bytes 1048576 | tf_op jit(solution)/shard_map/pallas_call | solution.py:275
  74.1 19.5 %collective-permute-start = (f32[336,128]{1,0:T(8,128)}, f32[336,128]{1,0:T(8,128)S(1)}, u32[]{:S(2)}, u32[]{:S(2)}) collective-permute-start(f32[336,128]{1,0:T(8,128)} %shard_map.75), channel_id=1, source_target_pairs={{0,1},{1,2},{2,3},{3,4},{4,5},{5,6},{6,7},{7,8},{8,9},{9,10},{10,1... | collective-permute-start | bytes 516104 | tf_op jit(solution)/shard_map/ppermute | solution.py:330
  93.6 19.3 %shard_map.74 = (bf16[16,336,128]{2,1,0:T(8,128)(2,1)}, f32[336,128]{1,0:T(8,128)}) custom-call(s32[35]{0:T(128)} %select_reduce_fusion.3.starts, s32[848]{0:T(1024)} %get-tuple-element.30.slot, s32[848]{0:T(1024)} %broadcast_add_fusion.src, bf16[17,336,128]{2,1,0:T(8,128)(2,1)} %get-tuple-element.23.near, bf16[17,336,128]{2,1,0:T(8,128)(2,1)} %get-tuple-element.24.far, ...), custom_call_target="tpu_custom_call" | custom-call | flops 5967446016 | bytes 17760256 | tf_op jit(solution)/shard_map/pallas_call | solution.py:275
  112.9 0.0 collective-permute-done
  112.9 1.6 %fusion.3 = bf16[16,336,128]{2,1,0:T(8,128)(2,1)} fusion(bf16[16,336,128]{2,1,0:T(8,128)(2,1)} %get-tuple-element.26, f32[336,128]{1,0:T(8,128)} %get-tuple-element.27, f32[336,128]{1,0:T(8,128)S(1)} %collective-permute-done), kind=kLoop, calls=%fused_computation.13 | loop fusion | flops 86016 | bytes 430080 | tf_op jit(solution)/shard_map/scatter | solution.py:333
  (2 shorter events, 0.0 us)
Async XLA Ops:
  74.1 38.8 %collective-permute-start = (f32[336,128]{1,0:T(8,128)}, f32[336,128]{1,0:T(8,128)S(1)}, u32[]{:S(2)}, u32[]{:S(2)}) collective-permute-start(f32[336,128]{1,0:T(8,128)} %shard_map.75), channel_id=1, source_target_pairs={{0,1},{1,2},{2,3},{3,4},{4,5},{5,6},{6,7},{7,8},{8,9},{9,10},{10,1... | collective-permute-start | bytes 516104 | tf_op jit(solution)/shard_map/ppermute | solution.py:330
where the time goes:
time: 114 us; the launch traced here: 115 us
  Pallas kernels  86.4 us (76%)
  starting transfers between devices  19.5 us (17%)
  other arithmetic  7.22 us (6%)
  local copies, waits for them, and re-layouts  1.4 us (1%)
    pallas_call x1, Pallas kernels, exchange(): pl.pallas_call(functools.partial(exchange_kernel, n, steps), out_shape=[j...  62.8 us
    pallas_call x2, Pallas kernels, products(): pl.pallas_call(functools.partial(product_kernel, first, last, n_rows, don...  23.5 us
    ppermute x1, starting transfers between devices, shards(): lax.ppermute(excess, 'srv', [(i, (i + 1) % servers) for i in range(server...  19.5 us
  transfers between devices with their start and end apart: 1, of which 0 were waited for; matrix products, arithmetic and copies ran while one was open for 0% of the time, Pallas kernels for 17%

commit v1 on v0

--- a/solution.py
+++ b/solution.py
@@ -60,7 +60,9 @@
     load.start()
 
     def partner(i):
-        return lax.rem(me + half + ((i + 1) // 2) * (2 * ((i + 1) % 2) - 1), n)
+        mine = (me // half) * half + lax.rem(me + i + 1, half)
+        other = (1 - me // half) * half + lax.rem(me + i + 1, half)
+        return jnp.where(i < half - 1, mine, other)
 
     barrier = pltpu.get_barrier_semaphore()
 

time: 114 us -> 111 us (0.974)
  the two profiles are of different devices: /device:TPU:7 before, /device:TPU:25 now
where the time goes in v1:
time: 111 us; the launch traced here: 110 us
  Pallas kernels  101 us (91%)
  other arithmetic  7.22 us (7%)
  local copies, waits for them, and re-layouts  1.4 us (1%)
    pallas_call x1, Pallas kernels, exchange(): pl.pallas_call(functools.partial(exchange_kernel, n, steps), out_shape=[j...  77.2 us
    pallas_call x2, Pallas kernels, products(): pl.pallas_call(functools.partial(product_kernel, first, last, n_rows, don...  23.9 us
  transfers between devices with their start and end apart: 1, of which 0 were waited for; matrix products, arithmetic and copies ran while one was open for 0% of the time, Pallas kernels for 18%

profile of v1, /device:TPU:25, one launch (start us, length us, event | category | flops | bytes accessed | tf_op | source)
XLA Modules:
  0.0 109.8 jit_solution(12685127020075563345)
XLA Ops:
  0.0 0.7 broadcast_compare_fusion
  0.7 0.7 fusion.10
  1.4 0.7 fusion.6
  2.1 0.1 convert_reduce_fusion.1
  2.2 0.3 convert_reduce_fusion
  2.6 0.6 select_reduce_fusion.3.starts
  3.2 0.1 select_reduce_fusion.2
  3.3 0.7 select_add_fusion
  4.0 1.1 select_reduce_fusion
  5.1 0.6 broadcast_add_fusion.src
  5.7 0.8 copy.10
  6.4 0.6 broadcast_in_dim.85.wanted
  7.1 77.2 %shard_map.73 = (bf16[17,336,128]{2,1,0:T(8,128)(2,1)}, bf16[17,336,128]{2,1,0:T(8,128)(2,1)}, f32[16,336,128]{2,1,0:T(8,128)}, f32[336,128]{1,0:T(8,128)}) custom-call(s32[12]{0:T(128)} %tile_count.1, s32[35]{0:T(128)} %select_reduce_fusion.3.starts, s32[848]{0:T(1024)} %get-tuple-element.30.slot, s32[848]{0:T(1024)} %broadcast_add_fusion.src, ...), custom_call_target="tpu_custom_call" | custom-call | tf_op jit(solution)/shard_map/pallas_call | solution.py:198
  84.3 4.2 %shard_map.75 = f32[336,128]{1,0:T(8,128)} custom-call(s32[35]{0:T(128)} %select_reduce_fusion.3.starts, s32[848]{0:T(1024)} %get-tuple-element.30.slot, s32[848]{0:T(1024)} %broadcast_add_fusion.src, bf16[17,336,128]{2,1,0:T(8,128)(2,1)} %get-tuple-element.23.near, bf16[17,336,128]{2,1,0:T(8,128)(2,1)} %get-tuple-element.24.far, ...), custom_call_target="tpu_custom_call" | custom-call | flops 352321536 | bytes 1048576 | tf_op jit(solution)/shard_map/pallas_call | solution.py:277
  88.5 0.1 collective-permute-start
  88.5 19.7 %shard_map.74 = (bf16[16,336,128]{2,1,0:T(8,128)(2,1)}, f32[336,128]{1,0:T(8,128)}) custom-call(s32[35]{0:T(128)} %select_reduce_fusion.3.starts, s32[848]{0:T(1024)} %get-tuple-element.30.slot, s32[848]{0:T(1024)} %broadcast_add_fusion.src, bf16[17,336,128]{2,1,0:T(8,128)(2,1)} %get-tuple-element.23.near, bf16[17,336,128]{2,1,0:T(8,128)(2,1)} %get-tuple-element.24.far, ...), custom_call_target="tpu_custom_call" | custom-call | flops 5967446016 | bytes 17760256 | tf_op jit(solution)/shard_map/pallas_call | solution.py:277
  108.2 0.0 collective-permute-done
  108.3 1.6 %fusion.3 = bf16[16,336,128]{2,1,0:T(8,128)(2,1)} fusion(bf16[16,336,128]{2,1,0:T(8,128)(2,1)} %get-tuple-element.26, f32[336,128]{1,0:T(8,128)} %get-tuple-element.27, f32[336,128]{1,0:T(8,128)S(1)} %collective-permute-done), kind=kLoop, calls=%fused_computation.13 | loop fusion | flops 86016 | bytes 430080 | tf_op jit(solution)/shard_map/scatter | solution.py:335
  (2 shorter events, 0.0 us)
Async XLA Ops:
  88.5 19.8 %collective-permute-start = (f32[336,128]{1,0:T(8,128)}, f32[336,128]{1,0:T(8,128)S(1)}, u32[]{:S(2)}, u32[]{:S(2)}) collective-permute-start(f32[336,128]{1,0:T(8,128)} %shard_map.75), channel_id=1, source_target_pairs={{0,1},{1,2},{2,3},{3,4},{4,5},{5,6},{6,7},{7,8},{8,9},{9,10},{10,1... | collective-permute-start | bytes 516104 | tf_op jit(solution)/shard_map/ppermute | solution.py:332
